TPU v7x, 32 devices: a whole 2x2x4 slice. The times are simulated.
32 devices in a mesh: ctx: 16 (over z, y, x), head: 2 (over core).
Axes of the slice: x: 2, y: 2, z: 4, core: 2. Of those that a mesh axis runs over, the one named last changes fastest.
Arguments:
- queries: bfloat16 [4096, 4, 256], P('ctx', 'head'), may hold values from -6 to 6
- token_keys: bfloat16 [4096, 4, 256], P('ctx', 'head'), may hold values from -6 to 6
- token_values: bfloat16 [4096, 4, 256], P('ctx', 'head'), may hold values from -6 to 6
- step_rates: float32 [4096, 4], P('ctx', 'head'), may hold values from 0.1 to 1
- counts: int32 [16], replicated, may hold values from 64 to 256, as said below
- fast_weights: float32 [4, 3, 256, 256], P('head'), may hold values from -0.375 to 0.375
- out_weight: bfloat16 [1024, 4096], P('head'), may hold values from -0.1875 to 0.1875
Outputs:
- layer_output: bfloat16 [4096, 4096], P('ctx', 'head')
Inputs may be any that keep to these rules, and one draw needn't show every extreme that they name: counts[i] tokens at the start of block i are valid, the rest are padding; some block is full and some holds exactly 64.
All inputs are finite; a program needn't handle non-finite values.
Results may differ from a plain program's by a relative error of at most 0.012.
The roundings to bfloat16 on the way count: a program that leaves them out, or rounds other values in their place, can miss the bound.
Values may be sent and summed in bfloat16 or wider, within the bound.
A program may use at most 64 MiB of HBM per device.

v0:
```python
import math

import jax
import jax.numpy as jnp
from jax import lax
from jax.sharding import PartitionSpec as P

SPAN = 2


def passed_along(value, axis, steps):
    count = lax.axis_size(axis)
    leading, last = (max(0, -steps), min(count, count - steps))
    return lax.ppermute(value, axis, [(source, source + steps) for source in range(leading, last)])


def silu_slope(pre_value):
    sigmoid_value = jax.nn.sigmoid(pre_value)
    return sigmoid_value * (1.0 + pre_value * (1.0 - sigmoid_value))


def refresh(old_rows, gradient_rows, token_total):
    updated = old_rows - gradient_rows / math.sqrt(token_total)
    old_norm = jnp.sqrt(jnp.sum(old_rows * old_rows, axis=-1, keepdims=True))
    fresh = (
        updated * old_norm / jnp.sqrt(jnp.sum(updated * updated, axis=-1, keepdims=True) + 1e-06)
    )
    return fresh.astype(jnp.bfloat16)


def shards(queries, token_keys, token_values, step_rates, counts, fast_weights, out_weight):
    tok_rows, head_local, head_width = queries.shape
    device_count = lax.axis_size("ctx")
    device_place = lax.axis_index("ctx")
    positions = jnp.arange(tok_rows, dtype=jnp.int32)
    own_count = lax.dynamic_index_in_dim(counts, device_place, 0, keepdims=False)
    valid_rows = (positions < own_count).astype(jnp.float32)
    weights_low = fast_weights.astype(jnp.bfloat16)
    gate_pre = jnp.einsum(
        "thi,hci->thc", token_keys, weights_low[:, 0], preferred_element_type=jnp.float32
    )
    up_pre = jnp.einsum(
        "thi,hci->thc", token_keys, weights_low[:, 1], preferred_element_type=jnp.float32
    )
    gate_act = jax.nn.silu(gate_pre)
    hidden = (gate_act * up_pre).astype(jnp.bfloat16)
    scaled = (
        (step_rates * valid_rows[:, None])[:, :, None] * token_values.astype(jnp.float32)
    ).astype(jnp.bfloat16)
    grad_down = -jnp.einsum("thd,thc->hdc", scaled, hidden, preferred_element_type=jnp.float32)
    back_hidden = -jnp.einsum(
        "thd,hdc->thc", scaled, weights_low[:, 2], preferred_element_type=jnp.float32
    )
    grad_gate = (back_hidden * up_pre * silu_slope(gate_pre)).astype(jnp.bfloat16)
    grad_up = (back_hidden * gate_act).astype(jnp.bfloat16)
    first_grad = jnp.einsum(
        "thc,thi->hci", grad_gate, token_keys, preferred_element_type=jnp.float32
    )
    second_grad = jnp.einsum(
        "thc,thi->hci", grad_up, token_keys, preferred_element_type=jnp.float32
    )
    local_grad = jnp.stack([first_grad, second_grad, grad_down], axis=1).reshape(-1, head_width)
    old_flat = fast_weights.reshape(-1, head_width)
    token_total = tok_rows * device_count
    grad_whole = lax.psum(local_grad, "ctx")
    new_flat = refresh(old_flat, grad_whole, token_total)
    new_weights = new_flat.reshape(head_local, 3, head_width, head_width)
    query_gate = jnp.einsum(
        "thi,hci->thc", queries, new_weights[:, 0], preferred_element_type=jnp.float32
    )
    query_up = jnp.einsum(
        "thi,hci->thc", queries, new_weights[:, 1], preferred_element_type=jnp.float32
    )
    query_hidden = (jax.nn.silu(query_gate) * query_up).astype(jnp.bfloat16)
    ttt_out = jnp.einsum(
        "thc,hdc->thd", query_hidden, new_weights[:, 2], preferred_element_type=jnp.float32
    )
    key_parts = []
    value_parts = []
    valid_parts = []
    for back_step in range(SPAN, 0, -1):
        moved_keys, moved_values = passed_along((token_keys, token_values), "ctx", back_step)
        source = device_place - back_step
        source_count = lax.dynamic_index_in_dim(counts, jnp.maximum(source, 0), 0, keepdims=False)
        valid_parts.append(((positions < source_count) & (source >= 0)).astype(jnp.float32))
        key_parts.append(moved_keys)
        value_parts.append(moved_values)
    key_parts.append(token_keys)
    value_parts.append(token_values)
    valid_parts.append(valid_rows)
    seen_keys = jnp.concatenate(key_parts, 0)
    seen_values = jnp.concatenate(value_parts, 0)
    seen_valid = jnp.concatenate(valid_parts, 0)
    window_len = SPAN * tok_rows
    distance = (
        window_len
        + positions[:, None]
        - jnp.arange(window_len + tok_rows, dtype=jnp.int32)[None, :]
    )
    scores = jnp.einsum(
        "thi,shi->hts", queries, seen_keys, preferred_element_type=jnp.float32
    ) / math.sqrt(head_width)
    allowed = (distance >= 0) & (distance < window_len) & (seen_valid[None, :] > 0.5)
    scores = jnp.where(allowed[None], scores, -1e30)
    top_score = jnp.max(scores, axis=-1, keepdims=True)
    expo = jnp.exp(scores - top_score)
    attention = (expo / jnp.sum(expo, axis=-1, keepdims=True)).astype(jnp.bfloat16)
    window_out = jnp.einsum(
        "hts,shd->thd", attention, seen_values, preferred_element_type=jnp.float32
    )
    features = ((ttt_out + window_out) * valid_rows[:, None, None]).astype(jnp.bfloat16)
    features = features.reshape(tok_rows, head_local * head_width)
    partial_out = jnp.dot(features, out_weight, preferred_element_type=jnp.float32)
    return lax.psum_scatter(
        partial_out.astype(jnp.bfloat16), "head", scatter_dimension=1, tiled=True
    )


def solution(mesh):
    in_specs = (
        P("ctx", "head", None),
        P("ctx", "head", None),
        P("ctx", "head", None),
        P("ctx", "head"),
        P(),
        P("head", None, None, None),
        P("head", None),
    )
    out_specs = P("ctx", "head")
    return jax.shard_map(shards, mesh=mesh, in_specs=in_specs, out_specs=out_specs, check_vma=False)
```

profile of v0, /device:TPU:9, one launch (start us, length us, event | category | flops | bytes accessed | tf_op | source)
XLA Modules:
  0.0 173.1 jit_solution(1435693653547176348)
XLA Ops:
  6.6 1.5 convolution_bitcast_fusion.4
  8.1 2.2 %convolution_bitcast_fusion.5 = f32[256,2,256]{2,0,1:T(8,128)} fusion(bf16[256,2,256]{2,1,0:T(2,128)(2,1)} %param.8, f32[2,3,256,256]{3,2,1,0:T(8,128)} %param.12), kind=kOutput, calls=%fused_computation.21 | convolution fusion | flops 67108864 | bytes 1048576 | tf_op jit(solution)/shard_map/thi,hci->thc/dot_general | solution.py:42
  10.3 0.7 fusion.60
  11.0 0.6 compare_convert_fusion
  12.7 0.4 convolution_bitcast_fusion.2
  13.0 0.7 copy-done.6
  13.7 0.4 convolution_bitcast_fusion.3
  14.1 0.3 fusion.4
  14.7 1.3 copy.42
  16.0 3.2 %collective-permute-start.2 = (bf16[256,2,256]{2,0,1:T(8,128)(2,1)S(1)}, bf16[256,2,256]{2,0,1:T(8,128)(2,1)}, u32[]{:S(2)}, u32[]{:S(2)}) collective-permute-start(bf16[256,2,256]{2,0,1:T(8,128)(2,1)S(1)} %copy.33), channel_id=1, source_target_pairs={{0,4},{2,6},{4,8},{6,10},{8,12},{10,14},{12,16},{14,18},{16,20},{1... | collective-permute-start | bytes 786440 | tf_op jit(solution)/shard_map/ppermute | solution.py:14
  19.2 3.1 %collective-permute-start.3 = (bf16[256,2,256]{2,0,1:T(8,128)(2,1)S(1)}, bf16[256,2,256]{2,0,1:T(8,128)(2,1)}, u32[]{:S(2)}, u32[]{:S(2)}) collective-permute-start(bf16[256,2,256]{2,0,1:T(8,128)(2,1)S(1)} %copy.33), channel_id=1, source_target_pairs={{0,2},{2,4},{4,6},{6,8},{8,10},{10,12},{12,14},{14,16},{16,18},{18... | collective-permute-start | bytes 786440 | tf_op jit(solution)/shard_map/ppermute | solution.py:14
  22.5 3.1 %collective-permute-start = (bf16[256,2,256]{0,2,1:T(8,128)(2,1)S(1)}, bf16[256,2,256]{0,2,1:T(8,128)(2,1)S(1)}, u32[]{:S(2)}, u32[]{:S(2)}) collective-permute-start(bf16[256,2,256]{0,2,1:T(8,128)(2,1)S(1)} %copy.47), channel_id=1, source_target_pairs={{0,4},{2,6},{4,8},{6,10},{8,12},{10,14},{12,16},{14,18},{16,20},{1... | collective-permute-start | bytes 786440 | tf_op jit(solution)/shard_map/ppermute | solution.py:14
  25.6 3.1 %collective-permute-start.1 = (bf16[256,2,256]{0,2,1:T(8,128)(2,1)S(1)}, bf16[256,2,256]{0,2,1:T(8,128)(2,1)}, u32[]{:S(2)}, u32[]{:S(2)}) collective-permute-start(bf16[256,2,256]{0,2,1:T(8,128)(2,1)S(1)} %copy.47), channel_id=1, source_target_pairs={{0,2},{2,4},{4,6},{6,8},{8,10},{10,12},{12,14},{14,16},{16,18},{18... | collective-permute-start | bytes 786440 | tf_op jit(solution)/shard_map/ppermute | solution.py:14
  28.8 1.3 and_convert_fusion
  30.7 8.8 %collective-permute-done.3 = bf16[256,2,256]{2,0,1:T(8,128)(2,1)} collective-permute-done((bf16[256,2,256]{2,0,1:T(8,128)(2,1)S(1)}, bf16[256,2,256]{2,0,1:T(8,128)(2,1)}, u32[]{:S(2)}, u32[]{:S(2)}) %collective-permute-start.3) | collective-permute-done | bytes 262176 | tf_op jit(solution)/shard_map/ppermute | solution.py:14
  39.5 2.8 %fusion.61 = (f32[2,256]{1,0:T(2,128)S(1)}, f32[2,256,768]{1,2,0:T(8,128)}) fusion(bf16[256,2,256]{2,0,1:T(8,128)(2,1)S(1)} %copy.33, bf16[256,2,256]{2,0,1:T(8,128)(2,1)} %collective-permute-done.3, bf16[256,2,256]{2,0,1:T(8,128)(2,1)} %collective-permute-done.2, pred[256,768]{0,1:T(8,128)(4,1)S(1)} %fusion.23, bf16[256,2,256]{2,1,0:T(2,128)(2,1)S(1)} %copy-done), kind=kOutput, calls=%fused_computation.86 | convolution fusion | flops 205259520 | bytes 2820096 | tf_op jit(solution)/shard_map/sub | solution.py:106
  42.4 104.6 %all-reduce.2.cloned.1.call-done = f32[1536,256]{1,0:T(8,128)} async-done(((f32[1536,256]{1,0:T(8,128)}), f32[1536,256]{1,0:T(8,128)}) %all-reduce.2.cloned.1.call-update) | async-done | bytes 1572880 | tf_op jit(solution)/shard_map/psum | solution.py:65
  146.9 1.8 %multiply_reduce_fusion = f32[1536]{0:T(1024)S(1)} fusion(f32[1536,256]{1,0:T(8,128)} %all-reduce.2.cloned.1.call-done, f32[2,3,256,256]{3,2,1,0:T(8,128)S(1)} %copy-done.1), kind=kLoop, calls=%fused_computation.9 | loop fusion | flops 1571328 | bytes 3151872 | tf_op jit(solution)/shard_map/reduce_sum | solution.py:26
  148.8 0.5 divide_convert_fusion.1
  149.6 0.5 fusion.9
  150.1 2.0 %fusion.7 = bf16[2,256,256]{2,1,0:T(8,128)(2,1)S(1)} fusion(f32[2,256,256]{2,1,0:T(8,128)S(1)} %fusion.9, bf16[256,2,256]{0,2,1:T(8,128)(2,1)S(1)} %copy.47, bf16[256,2,256]{0,2,1:T(8,128)(2,1)} %collective-permute-done.1, bf16[256,2,256]{0,2,1:T(8,128)(2,1)S(1)} %collective-permute-done, f32[2,256,768]{1,2,0:T(8,128)} %get-tuple-element.9, ...), kind=kOutput, calls=%fused_computation.25 | convolution fusion | flops 204865536 | bytes 3148800 | tf_op jit(solution)/shard_map/hts,shd->thd/dot_general | solution.py:108
  152.1 0.7 copy-done.3
  152.8 2.6 %convolution_convert_fusion = bf16[256,4096]{1,0:T(8,128)(2,1)} fusion(bf16[256,512]{0,1:T(8,128)(2,1)S(1)} %bitcast.74, bf16[512,4096]{1,0:T(8,128)(2,1)S(1)} %copy-done.3), kind=kOutput, calls=%fused_computation.1 | convolution fusion | flops 1074790400 | bytes 6553600 | tf_op jit(solution)/shard_map/dot_general | solution.py:113
  155.5 10.8 %reduce-scatter.2.cloned.1.call-done = bf16[256,2048]{1,0:T(8,128)(2,1)} async-done(((bf16[256,4096]{1,0:T(8,128)(2,1)}), bf16[256,2048]{1,0:T(8,128)(2,1)}) %reduce-scatter.2.cloned.1.call-update) | async-done | bytes 1048592 | tf_op jit(solution)/shard_map/reduce_scatter | solution.py:114
  (39 shorter events, 2.3 us)
Async XLA Ops:
  6.5 33.0 %copy-start = (bf16[256,2,256]{2,1,0:T(2,128)(2,1)S(1)}, bf16[256,2,256]{2,1,0:T(2,128)(2,1)}, u32[]{:S(2)}) copy-start(bf16[256,2,256]{2,1,0:T(2,128)(2,1)} %param.7) | copy-start | bytes 786436
  6.5 3.8 %copy-start.7 = (s32[16]{0:T(128)S(1)}, s32[16]{0:T(128)}, u32[]{:S(2)}) copy-start(s32[16]{0:T(128)} %param.11) | copy-start | bytes 196
  6.5 5.1 %copy-start.8 = (f32[256,2]{0,1:T(2,128)S(1)}, f32[256,2]{0,1:T(2,128)}, u32[]{:S(2)}) copy-start(f32[256,2]{0,1:T(2,128)} %param.10) | copy-start | bytes 6148
  6.5 5.3 %copy-start.5 = (bf16[256,2,256]{2,1,0:T(2,128)(2,1)S(1)}, bf16[256,2,256]{2,1,0:T(2,128)(2,1)}, u32[]{:S(2)}) copy-start(bf16[256,2,256]{2,1,0:T(2,128)(2,1)} %param.9) | copy-start | bytes 786436
  6.5 140.4 %all-reduce.2.cloned.1.call-start = ((), (), s32[]{:S(2)}) async-start(), calls=%async_computation.1 | async-start | bytes 3145728 | tf_op jit(solution)/shard_map/psum | solution.py:65
  6.6 5.7 %copy-start.1 = (f32[2,3,256,256]{3,2,1,0:T(8,128)S(1)}, f32[2,3,256,256]{3,2,1,0:T(8,128)}, u32[]{:S(2)}) copy-start(f32[2,3,256,256]{3,2,1,0:T(8,128)} %param.12) | copy-start | bytes 4718596
  8.1 4.5 %copy-start.4 = (bf16[256,2,256]{2,1,0:T(2,128)(2,1)S(1)}, bf16[256,2,256]{2,1,0:T(2,128)(2,1)}, u32[]{:S(2)}) copy-start(bf16[256,2,256]{2,1,0:T(2,128)(2,1)} %param.8) | copy-start | bytes 786436
  12.6 1.0 copy-start.6
  15.9 150.3 %reduce-scatter.2.cloned.1.call-start = ((), (), s32[]{:S(2)}) async-start(), calls=%async_computation.2 | async-start | bytes 3145728 | tf_op jit(solution)/shard_map/reduce_scatter | solution.py:114
  16.0 14.7 %collective-permute-start.2 = (bf16[256,2,256]{2,0,1:T(8,128)(2,1)S(1)}, bf16[256,2,256]{2,0,1:T(8,128)(2,1)}, u32[]{:S(2)}, u32[]{:S(2)}) collective-permute-start(bf16[256,2,256]{2,0,1:T(8,128)(2,1)S(1)} %copy.33), channel_id=1, source_target_pairs={{0,4},{2,6},{4,8},{6,10},{8,12},{10,14},{12,16},{14,18},{16,20},{1... | collective-permute-start | bytes 786440 | tf_op jit(solution)/shard_map/ppermute | solution.py:14
  19.2 20.4 %collective-permute-start.3 = (bf16[256,2,256]{2,0,1:T(8,128)(2,1)S(1)}, bf16[256,2,256]{2,0,1:T(8,128)(2,1)}, u32[]{:S(2)}, u32[]{:S(2)}) collective-permute-start(bf16[256,2,256]{2,0,1:T(8,128)(2,1)S(1)} %copy.33), channel_id=1, source_target_pairs={{0,2},{2,4},{4,6},{6,8},{8,10},{10,12},{12,14},{14,16},{16,18},{18... | collective-permute-start | bytes 786440 | tf_op jit(solution)/shard_map/ppermute | solution.py:14
  22.5 127.5 %collective-permute-start = (bf16[256,2,256]{0,2,1:T(8,128)(2,1)S(1)}, bf16[256,2,256]{0,2,1:T(8,128)(2,1)S(1)}, u32[]{:S(2)}, u32[]{:S(2)}) collective-permute-start(bf16[256,2,256]{0,2,1:T(8,128)(2,1)S(1)} %copy.47), channel_id=1, source_target_pairs={{0,4},{2,6},{4,8},{6,10},{8,12},{10,14},{12,16},{14,18},{16,20},{1... | collective-permute-start | bytes 786440 | tf_op jit(solution)/shard_map/ppermute | solution.py:14
  25.6 124.4 %collective-permute-start.1 = (bf16[256,2,256]{0,2,1:T(8,128)(2,1)S(1)}, bf16[256,2,256]{0,2,1:T(8,128)(2,1)}, u32[]{:S(2)}, u32[]{:S(2)}) collective-permute-start(bf16[256,2,256]{0,2,1:T(8,128)(2,1)S(1)} %copy.47), channel_id=1, source_target_pairs={{0,2},{2,4},{4,6},{6,8},{8,10},{10,12},{12,14},{14,16},{16,18},{18... | collective-permute-start | bytes 786440 | tf_op jit(solution)/shard_map/ppermute | solution.py:14
  146.9 1.9 %copy-start.2 = (f32[1536,256]{1,0:T(8,128)S(1)}, f32[1536,256]{1,0:T(8,128)}, u32[]{:S(2)}) copy-start(f32[1536,256]{1,0:T(8,128)} %all-reduce.2.cloned.1.call-done) | copy-start | bytes 4718596
  150.1 2.7 %copy-start.3 = (bf16[512,4096]{1,0:T(8,128)(2,1)S(1)}, bf16[512,4096]{1,0:T(8,128)(2,1)}, u32[]{:S(2)}) copy-start(bf16[512,4096]{1,0:T(8,128)(2,1)} %param.13) | copy-start | bytes 12582916
Sparse Core Ops, SparseCore 0:
  16.1 130.8 all-reduce.1
  155.6 10.6 reduce-scatter.1
where the time goes:
time: 174 us; the launch traced here: 173 us
  waiting for transfers between devices  124 us (71%)
  between operations  13.7 us (8%)
  matrix products  13.4 us (8%)
  starting transfers between devices  12.6 us (7%)
  other arithmetic  5.31 us (3%)
  local copies, waits for them, and re-layouts  3.91 us (2%)
    psum x1, waiting for transfers between devices, shards(): grad_whole = lax.psum(local_grad, 'ctx')  105 us
    ppermute x4, starting transfers between devices, passed_along(): lax.ppermute(value, axis, [(source, source + steps) for source in range(l...  12.5 us
    reduce_scatter x1, waiting for transfers between devices, shards(): lax.psum_scatter(partial_out.astype(jnp.bfloat16), 'head', scatter_dimens...  10.8 us
    ppermute x4, waiting for transfers between devices, passed_along(): lax.ppermute(value, axis, [(source, source + steps) for source in range(l...  8.82 us
  transfers between devices with their start and end apart: 6, of which 3 were waited for; matrix products, arithmetic and copies ran while one was open for 5% of the time, Pallas kernels for 0%

commit v1 on v0

--- a/solution.py
+++ b/solution.py
@@ -1,11 +1,21 @@
+import functools
 import math
 
 import jax
 import jax.numpy as jnp
 from jax import lax
+from jax.experimental import pallas as pl
+from jax.experimental.pallas import tpu as pltpu
 from jax.sharding import PartitionSpec as P
 
 SPAN = 2
+NT = (((1,), (1,)), ((), ()))
+NN = (((1,), (0,)), ((), ()))
+TN = (((0,), (0,)), ((), ()))
+
+
+def dot(a, b, dims):
+    return lax.dot_general(a, b, dims, preferred_element_type=jnp.float32)
 
 
 def passed_along(value, axis, steps):
@@ -28,7 +38,7 @@
     return fresh.astype(jnp.bfloat16)
 
 
-def shards(queries, token_keys, token_values, step_rates, counts, fast_weights, out_weight):
+def plain_shards(queries, token_keys, token_values, step_rates, counts, fast_weights, out_weight):
     tok_rows, head_local, head_width = queries.shape
     device_count = lax.axis_size("ctx")
     device_place = lax.axis_index("ctx")
@@ -116,6 +126,346 @@
     )
 
 
+def kernel(
+    n, plane, counts, q, k, v, rates, fw, ow, out,
+    grads, part_in, part, last_in, fresh, halo_k, halo_v, window, wide, feats,
+    p1_s, p1_r, p2_s, p2_r, g1_s, g1_r, g2_s, g2_r, far_s, far_r, near_s, near_r,
+    w_s, w_r, w_l, f_s, f_r,
+):
+    tok, width = q.shape
+    hs = fw.shape[-1]
+    heads = width // hs
+    depth = n // plane
+    wide_rows, rows = hs // plane, hs // n
+    cols = out.shape[1]
+    c, side = lax.axis_index("ctx"), lax.axis_index("head")
+    place, layer = lax.rem(c, plane), lax.div(c, plane)
+    even = lax.rem(c, 2) == 0
+
+    def in_plane(d):
+        return layer * plane + lax.rem(place + d, plane)
+
+    def in_line(d):
+        return lax.rem(layer + d, depth) * plane + place
+
+    def remote(src, dst, send, recv, **device):
+        return pltpu.make_async_remote_copy(
+            src, dst, send, recv, device_id=device, device_id_type=pl.DeviceIdType.MESH
+        )
+
+    barrier = pltpu.get_barrier_semaphore()
+
+    def greet(**device):
+        pl.semaphore_signal(
+            barrier, inc=1, device_id=device, device_id_type=pl.DeviceIdType.MESH
+        )
+
+    for d in range(1, plane):
+        greet(ctx=in_plane(d))
+    for d in range(1, depth):
+        greet(ctx=in_line(d))
+    greet(head=1 - side)
+
+    @pl.when(c >= 2)
+    def _():
+        greet(ctx=c - 2)
+
+    @pl.when(jnp.logical_not(even))
+    def _():
+        greet(ctx=c - 1)
+
+    @pl.when(even & (c >= 2))
+    def _():
+        greet(ctx=c + 1)
+
+    sends = (
+        plane + depth - 1
+        + jnp.where(c + 2 < n, 1, 0)
+        + jnp.where(even | (c >= 2), 1, 0)
+    )
+    pl.semaphore_wait(barrier, sends)
+
+    def far(i):
+        src, dst = ((k, halo_k), (v, halo_v))[i]
+        return remote(src, dst.at[0], far_s.at[i], far_r.at[i], ctx=c + 2)
+
+    def near(i):
+        src, dst = ((k, halo_k), (v, halo_v))[i]
+        return remote(src, dst.at[1], near_s.at[i], near_r.at[i], ctx=c + 1)
+
+    def forward(i):
+        buf = (halo_k, halo_v)[i]
+        return remote(buf.at[0], buf.at[1], near_s.at[i], near_r.at[i], ctx=c - 1)
+
+    @pl.when(c + 2 < n)
+    def _():
+        for i in range(2):
+            far(i).start()
+
+    @pl.when(even)
+    def _():
+        for i in range(2):
+            near(i).start()
+
+    @pl.when(c < 2)
+    def _():
+        halo_k[0] = jnp.zeros((tok, width), jnp.bfloat16)
+        halo_v[0] = jnp.zeros((tok, width), jnp.bfloat16)
+
+    @pl.when(c < 1)
+    def _():
+        halo_k[1] = jnp.zeros((tok, width), jnp.bfloat16)
+        halo_v[1] = jnp.zeros((tok, width), jnp.bfloat16)
+
+    w_other = remote(
+        ow.at[:, pl.ds(pl.multiple_of((1 - side) * cols, 128), cols)],
+        wide.at[pl.ds(width, width)],
+        w_s, w_r, head=1 - side,
+    )
+    w_own = pltpu.make_async_copy(
+        ow.at[:, pl.ds(pl.multiple_of(side * cols, 128), cols)], wide.at[pl.ds(0, width)], w_l
+    )
+    w_other.start()
+    w_own.start()
+
+    def span(h):
+        return slice(h * hs, (h + 1) * hs)
+
+    token_ids = lax.broadcasted_iota(jnp.int32, (tok, 1), 0)
+    valid = (token_ids < counts[c]).astype(jnp.float32)
+
+    def wide_at(index):
+        return pl.ds(pl.multiple_of(index * wide_rows, wide_rows), wide_rows)
+
+    def row_at(layer_index):
+        return pl.ds(pl.multiple_of(place * wide_rows + layer_index * rows, rows), rows)
+
+    def plane_sum(h, d):
+        return remote(
+            grads.at[h, :, wide_at(lax.rem(place + d, plane))],
+            part_in.at[h, d - 1],
+            p1_s.at[h, d - 1], p1_r.at[h, d - 1], ctx=in_plane(d),
+        )
+
+    def line_sum(h, d):
+        other = lax.rem(layer + d, depth)
+        return remote(
+            part.at[h, :, pl.ds(pl.multiple_of(other * rows, rows), rows)],
+            last_in.at[h, d - 1],
+            p2_s.at[h, d - 1], p2_r.at[h, d - 1], ctx=in_line(d),
+        )
+
+    def line_gather(h, d, source):
+        held = fresh.at[h, :, row_at(source)]
+        return remote(held, held, g1_s.at[h, d - 1], g1_r.at[h, d - 1], ctx=in_line(d))
+
+    def plane_gather(h, d, source):
+        held = fresh.at[h, :, wide_at(source)]
+        return remote(held, held, g2_s.at[h, d - 1], g2_r.at[h, d - 1], ctx=in_plane(d))
+
+    def line_source(d):
+        return lax.rem(layer + depth - d, depth)
+
+    def plane_source(d):
+        return lax.rem(place + plane - d, plane)
+
+    for h in range(heads):
+        keys = k[:, span(h)]
+        low = [fw[h, m].astype(jnp.bfloat16) for m in range(3)]
+        gate_pre = dot(keys, low[0], NT)
+        up_pre = dot(keys, low[1], NT)
+        sig = jax.nn.sigmoid(gate_pre)
+        gate_act = gate_pre * sig
+        hidden = (gate_act * up_pre).astype(jnp.bfloat16)
+        scaled = ((rates[:, h : h + 1] * valid) * v[:, span(h)].astype(jnp.float32)).astype(
+            jnp.bfloat16
+        )
+        back = -dot(scaled, low[2], NN)
+        grad_gate = (back * up_pre * (sig * (1.0 + gate_pre * (1.0 - sig)))).astype(jnp.bfloat16)
+        grad_up = (back * gate_act).astype(jnp.bfloat16)
+        grads[h, 0] = dot(grad_gate, keys, TN).astype(jnp.bfloat16)
+        grads[h, 1] = dot(grad_up, keys, TN).astype(jnp.bfloat16)
+        grads[h, 2] = (-dot(scaled, hidden, TN)).astype(jnp.bfloat16)
+        for d in range(1, plane):
+            plane_sum(h, d).start()
+
+    for h in range(heads):
+        total = grads[h, :, wide_at(place)].astype(jnp.float32)
+        for d in range(1, plane):
+            plane_sum(h, d).wait_recv()
+            total += part_in[h, d - 1].astype(jnp.float32)
+        part[h] = total.astype(jnp.bfloat16)
+        for d in range(1, depth):
+            line_sum(h, d).start()
+
+    @pl.when(c >= 2)
+    def _():
+        for i in range(2):
+            far(i).wait_recv()
+
+            @pl.when(jnp.logical_not(even))
+            def _():
+                forward(i).start()
+
+    for h in range(heads):
+        total = part[h, :, pl.ds(pl.multiple_of(layer * rows, rows), rows)].astype(jnp.float32)
+        for d in range(1, depth):
+            line_sum(h, d).wait_recv()
+            total += last_in[h, d - 1].astype(jnp.float32)
+        fresh[h, :, row_at(layer)] = refresh(fw[h, :, row_at(layer)], total, tok * n)
+        for d in range(1, depth):
+            line_gather(h, d, layer).start()
+
+    for h in range(heads):
+        for d in range(1, depth):
+            line_gather(h, d, line_source(d)).wait_recv()
+        for d in range(1, plane):
+            plane_gather(h, d, place).start()
+
+    @pl.when(c >= 1)
+    def _():
+        for i in range(2):
+            near(i).wait_recv()
+
+    key_ids = lax.broadcasted_iota(jnp.int32, (tok, tok), 1)
+    row_ids = lax.broadcasted_iota(jnp.int32, (tok, tok), 0)
+    count_2 = jnp.where(c >= 2, counts[jnp.maximum(c - 2, 0)], 0)
+    count_1 = jnp.where(c >= 1, counts[jnp.maximum(c - 1, 0)], 0)
+    allowed = (
+        (key_ids > row_ids) & (key_ids < count_2),
+        key_ids < count_1,
+        (key_ids <= row_ids) & (key_ids < counts[c]),
+    )
+    for h in range(heads):
+        asked = q[:, span(h)]
+        scores = [
+            jnp.where(ok, dot(asked, held, NT) / math.sqrt(hs), -1e30)
+            for ok, held in zip(
+                allowed, (halo_k[0, :, span(h)], halo_k[1, :, span(h)], k[:, span(h)])
+            )
+        ]
+        top = functools.reduce(
+            jnp.maximum, [jnp.max(s, axis=-1, keepdims=True) for s in scores]
+        )
+        expo = [jnp.exp(s - top) for s in scores]
+        norm = sum(jnp.sum(e, axis=-1, keepdims=True) for e in expo)
+        window[:, span(h)] = sum(
+            dot((e / norm).astype(jnp.bfloat16), held, NN)
+            for e, held in zip(
+                expo, (halo_v[0, :, span(h)], halo_v[1, :, span(h)], v[:, span(h)])
+            )
+        )
+
+    def feature_swap(h):
+        return remote(
+            feats.at[:, span(h)],
+            feats.at[:, slice(width + h * hs, width + (h + 1) * hs)],
+            f_s.at[h], f_r.at[h], head=1 - side,
+        )
+
+    for h in range(heads):
+        for d in range(1, plane):
+            plane_gather(h, d, plane_source(d)).wait_recv()
+        asked = q[:, span(h)]
+        query_gate = dot(asked, fresh[h, 0], NT)
+        query_up = dot(asked, fresh[h, 1], NT)
+        query_hidden = (query_gate * jax.nn.sigmoid(query_gate) * query_up).astype(jnp.bfloat16)
+        ttt_out = dot(query_hidden, fresh[h, 2], NT)
+        feats[:, span(h)] = ((ttt_out + window[:, span(h)]) * valid).astype(jnp.bfloat16)
+        feature_swap(h).start()
+
+    w_own.wait()
+    w_other.wait_recv()
+    for h in range(heads):
+        feature_swap(h).wait_recv()
+    all_features = feats[...]
+    step = min(cols, 512)
+    for at in range(0, cols, step):
+        out[:, at : at + step] = dot(all_features, wide[:, at : at + step], NN).astype(out.dtype)
+
+    w_other.wait_send()
+    for h in range(heads):
+        feature_swap(h).wait_send()
+        for d in range(1, plane):
+            plane_sum(h, d).wait_send()
+            plane_gather(h, d, place).wait_send()
+        for d in range(1, depth):
+            line_sum(h, d).wait_send()
+            line_gather(h, d, layer).wait_send()
+
+    @pl.when(c + 2 < n)
+    def _():
+        for i in range(2):
+            far(i).wait_send()
+
+    @pl.when(even)
+    def _():
+        for i in range(2):
+            near(i).wait_send()
+
+    @pl.when(jnp.logical_not(even) & (c >= 2))
+    def _():
+        for i in range(2):
+            forward(i).wait_send()
+
+
+def shards(queries, token_keys, token_values, step_rates, counts, fast_weights, out_weight, *, n, plane):
+    tok, heads, hs = queries.shape
+    width = heads * hs
+    depth = n // plane
+    cols = out_weight.shape[1] // 2
+    vmem, dma = pltpu.VMEM, pltpu.SemaphoreType.DMA
+    bf16, f32 = jnp.bfloat16, jnp.float32
+    wide_rows, rows = hs // plane, hs // n
+    in_vmem = pl.BlockSpec(memory_space=pltpu.VMEM)
+    return pl.pallas_call(
+        functools.partial(kernel, n, plane),
+        out_shape=jax.ShapeDtypeStruct((tok, cols), bf16),
+        in_specs=[pl.BlockSpec(memory_space=pltpu.SMEM)]
+        + [in_vmem] * 5
+        + [pl.BlockSpec(memory_space=pltpu.HBM)],
+        out_specs=in_vmem,
+        scratch_shapes=[
+            vmem((heads, 3, hs, hs), bf16),
+            vmem((heads, plane - 1, 3, wide_rows, hs), bf16),
+            vmem((heads, 3, wide_rows, hs), bf16),
+            vmem((heads, depth - 1, 3, rows, hs), bf16),
+            vmem((heads, 3, hs, hs), bf16),
+            vmem((2, tok, width), bf16),
+            vmem((2, tok, width), bf16),
+            vmem((tok, width), f32),
+            vmem((2 * width, cols), bf16),
+            vmem((tok, 2 * width), bf16),
+            dma((heads, plane - 1)), dma((heads, plane - 1)),
+            dma((heads, depth - 1)), dma((heads, depth - 1)),
+            dma((heads, depth - 1)), dma((heads, depth - 1)),
+            dma((heads, plane - 1)), dma((heads, plane - 1)),
+            dma((2,)), dma((2,)), dma((2,)), dma((2,)),
+            dma, dma, dma,
+            dma((heads,)), dma((heads,)),
+        ],
+        compiler_params=pltpu.CompilerParams(
+            collective_id=0, has_side_effects=True, vmem_limit_bytes=48 * 1024 * 1024
+        ),
+        name="layer",
+    )(
+        counts,
+        queries.reshape(tok, width),
+        token_keys.reshape(tok, width),
+        token_values.reshape(tok, width),
+        step_rates,
+        fast_weights,
+        out_weight,
+    )
+
+
+def fitting_plane(n, hs):
+    if n % 2 or hs % (16 * n):
+        return 0
+    plane = max(p for p in range(1, math.isqrt(n) + 1) if n % p == 0)
+    return plane if plane > 1 else 0
+
+
 def solution(mesh):
     in_specs = (
         P("ctx", "head", None),
@@ -127,4 +477,14 @@
         P("head", None),
     )
     out_specs = P("ctx", "head")
-    return jax.shard_map(shards, mesh=mesh, in_specs=in_specs, out_specs=out_specs, check_vma=False)
+    n = mesh.shape["ctx"]
+
+    def layer(*args):
+        hs = args[5].shape[-1]
+        plane = fitting_plane(n, hs) if mesh.shape["head"] == 2 else 0
+        body = functools.partial(shards, n=n, plane=plane) if plane else plain_shards
+        return jax.shard_map(
+            body, mesh=mesh, in_specs=in_specs, out_specs=out_specs, check_vma=False
+        )(*args)
+
+    return layer

time: 174 us -> 58.2 us (0.33)
  waiting for transfers between devices: 124 us -> 0 us
  Pallas kernels: 0 us -> 51.1 us
  between operations: 13.7 us -> 0.04 us
  matrix products: 13.4 us -> 0 us
  starting transfers between devices: 12.6 us -> 0 us
  other arithmetic: 5.31 us -> 0 us
  local copies, waits for them, and re-layouts: 3.91 us -> 6.79 us
    psum x1 -> x0, waiting for transfers between devices: 105 us -> none  [shards(): grad_whole = lax.psum(local_grad, 'ctx')]
    pallas_call x0 -> x1, Pallas kernels: none -> 51.1 us  [shards(): pl.pallas_call(functools.partial(kernel, n, plane), out_shape=jax.ShapeDt...]
    ppermute x4 -> x0, starting transfers between devices: 12.5 us -> none  [passed_along(): lax.ppermute(value, axis, [(source, source + steps) for source in range(l...]
    reduce_scatter x1 -> x0, waiting for transfers between devices: 10.8 us -> none  [shards(): lax.psum_scatter(partial_out.astype(jnp.bfloat16), 'head', scatter_dimens...]
    dot_general x10 -> x0, matrix products: 10.5 us -> none  [the longest x1 2.64 us: shards(): jnp.dot(features, out_weight, preferred_element_type=jnp.float32)]
    ppermute x4 -> x0, waiting for transfers between devices: 8.82 us -> none  [passed_along(): lax.ppermute(value, axis, [(source, source + steps) for source in range(l...]
    unnamed x20 -> x9, local copies, waits for them, and re-layouts: 1.67 us -> 6.79 us
    sub x1 -> x0, matrix products: 2.83 us -> none  [shards(): expo = jnp.exp(scores - top_score)]
  transfers between devices with their start and end apart: 6 -> 0, of which waited for: 3 -> 0; matrix products, arithmetic and copies ran while one was open for 5% -> 0% of each run, Pallas kernels for 0% -> 0%
where the time goes in v1:
time: 58.2 us; the launch traced here: 57.9 us
  Pallas kernels  51.1 us (88%)
  local copies, waits for them, and re-layouts  6.79 us (12%)
    pallas_call x1, Pallas kernels, shards(): pl.pallas_call(functools.partial(kernel, n, plane), out_shape=jax.ShapeDt...  51.1 us
    unnamed x9, local copies, waits for them, and re-layouts  6.79 us

profile of v1, /device:TPU:9, one launch (start us, length us, event | category | flops | bytes accessed | tf_op | source)
XLA Modules:
  0.0 57.9 jit_solution(1356446038324519551)
XLA Ops:
  0.0 0.8 %copy.8.rates = f32[256,2]{1,0:T(8,128)S(1)} copy(f32[256,2]{0,1:T(2,128)} %param.10) | data formatting | bytes 4096 | tf_op args[3]
  0.8 1.0 %copy.9 = bf16[32,8,2,256]{3,1,2,0:T(8,128)(2,1)S(1)} copy(bf16[32,8,2,256]{3,2,1,0:T(2,128)(2,1)} %bitcast.9) | data formatting | bytes 524288
  1.8 1.0 %copy.10 = bf16[32,8,2,256]{3,1,2,0:T(8,128)(2,1)S(1)} copy(bf16[32,8,2,256]{3,2,1,0:T(2,128)(2,1)} %bitcast.10) | data formatting | bytes 524288
  2.8 1.0 %copy.11 = bf16[32,8,2,256]{3,1,2,0:T(8,128)(2,1)S(1)} copy(bf16[32,8,2,256]{3,2,1,0:T(2,128)(2,1)} %bitcast.11) | data formatting | bytes 524288
  3.8 0.0 copy-start
  3.8 1.4 %copy-done = f32[2,3,256,256]{3,2,1,0:T(8,128)S(1)} copy-done((f32[2,3,256,256]{3,2,1,0:T(8,128)S(1)}, f32[2,3,256,256]{3,2,1,0:T(8,128)}, u32[]{:S(2)}) %copy-start) | copy-done | bytes 1572888
  5.2 0.0 copy-start.1
  5.2 0.7 %copy-done.1 = s32[16]{0:T(128)S(1)} copy-done((s32[16]{0:T(128)S(1)}, s32[16]{0:T(128)}, u32[]{:S(2)}) %copy-start.1) | copy-done | bytes 88
  5.8 51.1 %layer.1 = bf16[256,2048]{1,0:T(8,128)(2,1)S(1)} custom-call(s32[16]{0:T(128)S(1)} %copy-done.1, bf16[256,512]{1,0:T(8,128)(2,1)S(1)} %bitcast.6, bf16[256,512]{1,0:T(8,128)(2,1)S(1)} %bitcast.7, bf16[256,512]{1,0:T(8,128)(2,1)S(1)} %bitcast.8, f32[256,2]{1,0:T(8,128)S(1)} %copy.8.rates, f32[2,3,256,256]{3,2,1,0:T(8,128)S(1)} %copy-done, bf16[512,4096]{1,0:T(8,128)(2,1)} %ow.1), custom_call_target="tpu_custom_call" | custom-call | tf_op jit(solution)/shard_map/layer/pallas_call | solution.py:421
  56.9 1.0 %copy.13 = bf16[256,2048]{1,0:T(8,128)(2,1)} copy(bf16[256,2048]{1,0:T(8,128)(2,1)S(1)} %layer.1) | data formatting | bytes 2097152
Async XLA Ops:
  3.8 1.4 %copy-start = (f32[2,3,256,256]{3,2,1,0:T(8,128)S(1)}, f32[2,3,256,256]{3,2,1,0:T(8,128)}, u32[]{:S(2)}) copy-start(f32[2,3,256,256]{3,2,1,0:T(8,128)} %fw.1) | copy-start | bytes 4718596
  5.2 0.7 %copy-start.1 = (s32[16]{0:T(128)S(1)}, s32[16]{0:T(128)}, u32[]{:S(2)}) copy-start(s32[16]{0:T(128)} %counts.1) | copy-start | bytes 196

commit v2 on v1

--- a/solution.py
+++ b/solution.py
@@ -9,6 +9,8 @@
 from jax.sharding import PartitionSpec as P
 
 SPAN = 2
+FIRST_AT = {"entry": (0, 1), "lined 0": (2,), "lined 1": (3,)}
+SECOND_AT = {"summed 0": (0,), "summed 1": (1,), "fresh 0": (2,), "fresh 1": (3,)}
 NT = (((1,), (1,)), ((), ()))
 NN = (((1,), (0,)), ((), ()))
 TN = (((0,), (0,)), ((), ()))
@@ -127,14 +129,13 @@
 
 
 def kernel(
-    n, plane, counts, q, k, v, rates, fw, ow, out,
-    grads, part_in, part, last_in, fresh, halo_k, halo_v, window, wide, feats,
+    n, plane, counts_in, q_in, k_in, v_in, rates_in, fw_in, ow, out,
+    counts, q, k, v, rates, fw, in_s, grads, part_in, part, last_in, fresh, halo_k, halo_v, window, wide, feats,
     p1_s, p1_r, p2_s, p2_r, g1_s, g1_r, g2_s, g2_r, far_s, far_r, near_s, near_r,
     w_s, w_r, w_l, f_s, f_r,
 ):
-    tok, width = q.shape
-    hs = fw.shape[-1]
-    heads = width // hs
+    tok, heads, hs = k.shape
+    width = heads * hs
     depth = n // plane
     wide_rows, rows = hs // plane, hs // n
     cols = out.shape[1]
@@ -153,6 +154,17 @@
             src, dst, send, recv, device_id=device, device_id_type=pl.DeviceIdType.MESH
         )
 
+    fetch_counts = pltpu.make_async_copy(counts_in, counts, in_s.at[0])
+    fetch_rates = pltpu.make_async_copy(rates_in, rates, in_s.at[1])
+    fetch_q = pltpu.make_async_copy(q_in, q, in_s.at[2])
+    fetch_fw = [
+        pltpu.make_async_copy(fw_in.at[h], fw.at[h], in_s.at[3 + h]) for h in range(heads)
+    ]
+    fetch_k = pltpu.make_async_copy(k_in, k, in_s.at[3 + heads])
+    fetch_v = pltpu.make_async_copy(v_in, v, in_s.at[4 + heads])
+    for copy in (fetch_k, fetch_v, *fetch_fw, fetch_counts, fetch_rates, fetch_q):
+        copy.start()
+
     barrier = pltpu.get_barrier_semaphore()
 
     def greet(**device):
@@ -185,37 +197,55 @@
     )
     pl.semaphore_wait(barrier, sends)
 
+    half = tok // 2
+
+    def piece(i):
+        at = pl.ds((i // 2) * half, half)
+        return ((k_in, halo_k), (v_in, halo_v))[i % 2] + (at,)
+
     def far(i):
-        src, dst = ((k, halo_k), (v, halo_v))[i]
-        return remote(src, dst.at[0], far_s.at[i], far_r.at[i], ctx=c + 2)
+        src, dst, at = piece(i)
+        return remote(src.at[at], dst.at[0, at], far_s.at[i], far_r.at[i], ctx=c + 2)
 
     def near(i):
-        src, dst = ((k, halo_k), (v, halo_v))[i]
-        return remote(src, dst.at[1], near_s.at[i], near_r.at[i], ctx=c + 1)
+        src, dst, at = piece(i)
+        return remote(src.at[at], dst.at[1, at], near_s.at[i], near_r.at[i], ctx=c + 1)
 
     def forward(i):
-        buf = (halo_k, halo_v)[i]
-        return remote(buf.at[0], buf.at[1], near_s.at[i], near_r.at[i], ctx=c - 1)
-
-    @pl.when(c + 2 < n)
-    def _():
-        for i in range(2):
-            far(i).start()
-
-    @pl.when(even)
-    def _():
-        for i in range(2):
-            near(i).start()
+        _, buf, at = piece(i)
+        return remote(buf.at[0, at], buf.at[1, at], near_s.at[i], near_r.at[i], ctx=c - 1)
+
+    def send_halo(point):
+        firsts, seconds = FIRST_AT.get(point, ()), SECOND_AT.get(point, ())
+        if firsts:
+            @pl.when(c + 2 < n)
+            def _():
+                for i in firsts:
+                    far(i).start()
+
+            @pl.when(even)
+            def _():
+                for i in firsts:
+                    near(i).start()
+
+        if seconds:
+            @pl.when(jnp.logical_not(even) & (c >= 2))
+            def _():
+                for i in seconds:
+                    far(i).wait_recv()
+                    forward(i).start()
+
+    send_halo("entry")
 
     @pl.when(c < 2)
     def _():
-        halo_k[0] = jnp.zeros((tok, width), jnp.bfloat16)
-        halo_v[0] = jnp.zeros((tok, width), jnp.bfloat16)
+        halo_k[0] = jnp.zeros((tok, heads, hs), jnp.bfloat16)
+        halo_v[0] = jnp.zeros((tok, heads, hs), jnp.bfloat16)
 
     @pl.when(c < 1)
     def _():
-        halo_k[1] = jnp.zeros((tok, width), jnp.bfloat16)
-        halo_v[1] = jnp.zeros((tok, width), jnp.bfloat16)
+        halo_k[1] = jnp.zeros((tok, heads, hs), jnp.bfloat16)
+        halo_v[1] = jnp.zeros((tok, heads, hs), jnp.bfloat16)
 
     w_other = remote(
         ow.at[:, pl.ds(pl.multiple_of((1 - side) * cols, 128), cols)],
@@ -231,6 +261,10 @@
     def span(h):
         return slice(h * hs, (h + 1) * hs)
 
+    fetch_counts.wait()
+    fetch_rates.wait()
+    fetch_k.wait()
+    fetch_v.wait()
     token_ids = lax.broadcasted_iota(jnp.int32, (tok, 1), 0)
     valid = (token_ids < counts[c]).astype(jnp.float32)
 
@@ -270,14 +304,16 @@
         return lax.rem(place + plane - d, plane)
 
     for h in range(heads):
-        keys = k[:, span(h)]
+        fetch_fw[h].wait()
+        keys = k[:, h, :]
+        rate = jnp.broadcast_to(rates[h : h + 1, :], (8, tok)).T[:, 0:1]
         low = [fw[h, m].astype(jnp.bfloat16) for m in range(3)]
         gate_pre = dot(keys, low[0], NT)
         up_pre = dot(keys, low[1], NT)
         sig = jax.nn.sigmoid(gate_pre)
         gate_act = gate_pre * sig
         hidden = (gate_act * up_pre).astype(jnp.bfloat16)
-        scaled = ((rates[:, h : h + 1] * valid) * v[:, span(h)].astype(jnp.float32)).astype(
+        scaled = ((rate * valid) * v[:, h, :].astype(jnp.float32)).astype(
             jnp.bfloat16
         )
         back = -dot(scaled, low[2], NN)
@@ -288,6 +324,7 @@
         grads[h, 2] = (-dot(scaled, hidden, TN)).astype(jnp.bfloat16)
         for d in range(1, plane):
             plane_sum(h, d).start()
+        send_halo(f"summed {h}")
 
     for h in range(heads):
         total = grads[h, :, wide_at(place)].astype(jnp.float32)
@@ -297,15 +334,7 @@
         part[h] = total.astype(jnp.bfloat16)
         for d in range(1, depth):
             line_sum(h, d).start()
-
-    @pl.when(c >= 2)
-    def _():
-        for i in range(2):
-            far(i).wait_recv()
-
-            @pl.when(jnp.logical_not(even))
-            def _():
-                forward(i).start()
+        send_halo(f"lined {h}")
 
     for h in range(heads):
         total = part[h, :, pl.ds(pl.multiple_of(layer * rows, rows), rows)].astype(jnp.float32)
@@ -315,16 +344,25 @@
         fresh[h, :, row_at(layer)] = refresh(fw[h, :, row_at(layer)], total, tok * n)
         for d in range(1, depth):
             line_gather(h, d, layer).start()
+        send_halo(f"fresh {h}")
 
     for h in range(heads):
         for d in range(1, depth):
             line_gather(h, d, line_source(d)).wait_recv()
         for d in range(1, plane):
             plane_gather(h, d, place).start()
+        send_halo(f"gathered {h}")
+
+    fetch_q.wait()
+
+    @pl.when(even & (c >= 2))
+    def _():
+        for i in range(4):
+            far(i).wait_recv()
 
     @pl.when(c >= 1)
     def _():
-        for i in range(2):
+        for i in range(4):
             near(i).wait_recv()
 
     key_ids = lax.broadcasted_iota(jnp.int32, (tok, tok), 1)
@@ -337,11 +375,11 @@
         (key_ids <= row_ids) & (key_ids < counts[c]),
     )
     for h in range(heads):
-        asked = q[:, span(h)]
+        asked = q[:, h, :]
         scores = [
             jnp.where(ok, dot(asked, held, NT) / math.sqrt(hs), -1e30)
             for ok, held in zip(
-                allowed, (halo_k[0, :, span(h)], halo_k[1, :, span(h)], k[:, span(h)])
+                allowed, (halo_k[0, :, h, :], halo_k[1, :, h, :], k[:, h, :])
             )
         ]
         top = functools.reduce(
@@ -352,7 +390,7 @@
         window[:, span(h)] = sum(
             dot((e / norm).astype(jnp.bfloat16), held, NN)
             for e, held in zip(
-                expo, (halo_v[0, :, span(h)], halo_v[1, :, span(h)], v[:, span(h)])
+                expo, (halo_v[0, :, h, :], halo_v[1, :, h, :], v[:, h, :])
             )
         )
 
@@ -366,7 +404,7 @@
     for h in range(heads):
         for d in range(1, plane):
             plane_gather(h, d, plane_source(d)).wait_recv()
-        asked = q[:, span(h)]
+        asked = q[:, h, :]
         query_gate = dot(asked, fresh[h, 0], NT)
         query_up = dot(asked, fresh[h, 1], NT)
         query_hidden = (query_gate * jax.nn.sigmoid(query_gate) * query_up).astype(jnp.bfloat16)
@@ -395,17 +433,17 @@
 
     @pl.when(c + 2 < n)
     def _():
-        for i in range(2):
+        for i in range(4):
             far(i).wait_send()
 
     @pl.when(even)
     def _():
-        for i in range(2):
+        for i in range(4):
             near(i).wait_send()
 
     @pl.when(jnp.logical_not(even) & (c >= 2))
     def _():
-        for i in range(2):
+        for i in range(4):
             forward(i).wait_send()
 
 
@@ -417,22 +455,28 @@
     vmem, dma = pltpu.VMEM, pltpu.SemaphoreType.DMA
     bf16, f32 = jnp.bfloat16, jnp.float32
     wide_rows, rows = hs // plane, hs // n
+    in_hbm = pl.BlockSpec(memory_space=pltpu.HBM)
     in_vmem = pl.BlockSpec(memory_space=pltpu.VMEM)
     return pl.pallas_call(
         functools.partial(kernel, n, plane),
         out_shape=jax.ShapeDtypeStruct((tok, cols), bf16),
-        in_specs=[pl.BlockSpec(memory_space=pltpu.SMEM)]
-        + [in_vmem] * 5
-        + [pl.BlockSpec(memory_space=pltpu.HBM)],
+        in_specs=[in_hbm] * 7,
         out_specs=in_vmem,
         scratch_shapes=[
+            pltpu.SMEM(counts.shape, jnp.int32),
+            vmem(queries.shape, bf16),
+            vmem(queries.shape, bf16),
+            vmem(queries.shape, bf16),
+            vmem((heads, tok), f32),
+            vmem(fast_weights.shape, f32),
+            dma((5 + heads,)),
             vmem((heads, 3, hs, hs), bf16),
             vmem((heads, plane - 1, 3, wide_rows, hs), bf16),
             vmem((heads, 3, wide_rows, hs), bf16),
             vmem((heads, depth - 1, 3, rows, hs), bf16),
             vmem((heads, 3, hs, hs), bf16),
-            vmem((2, tok, width), bf16),
-            vmem((2, tok, width), bf16),
+            vmem((2, tok, heads, hs), bf16),
+            vmem((2, tok, heads, hs), bf16),
             vmem((tok, width), f32),
             vmem((2 * width, cols), bf16),
             vmem((tok, 2 * width), bf16),
@@ -440,20 +484,20 @@
             dma((heads, depth - 1)), dma((heads, depth - 1)),
             dma((heads, depth - 1)), dma((heads, depth - 1)),
             dma((heads, plane - 1)), dma((heads, plane - 1)),
-            dma((2,)), dma((2,)), dma((2,)), dma((2,)),
+            dma((4,)), dma((4,)), dma((4,)), dma((4,)),
             dma, dma, dma,
             dma((heads,)), dma((heads,)),
         ],
         compiler_params=pltpu.CompilerParams(
-            collective_id=0, has_side_effects=True, vmem_limit_bytes=48 * 1024 * 1024
+            collective_id=0, has_side_effects=True, vmem_limit_bytes=60 * 1024 * 1024
         ),
         name="layer",
     )(
         counts,
-        queries.reshape(tok, width),
-        token_keys.reshape(tok, width),
-        token_values.reshape(tok, width),
-        step_rates,
+        queries,
+        token_keys,
+        token_values,
+        step_rates.T,
         fast_weights,
         out_weight,
     )

time: 58.2 us -> 48.8 us (0.84)
  Pallas kernels: 51.1 us -> 46.2 us
  local copies, waits for them, and re-layouts: 6.79 us -> 2.3 us
    pallas_call x1, Pallas kernels: 51.1 us -> 46.2 us  [shards(): pl.pallas_call(functools.partial(kernel, n, plane), out_shape=jax.ShapeDt...]
    unnamed x9 -> x1, local copies, waits for them, and re-layouts: 6.79 us -> 2.3 us
where the time goes in v2:
time: 48.8 us; the launch traced here: 48.5 us
  Pallas kernels  46.2 us (95%)
  local copies, waits for them, and re-layouts  2.3 us (5%)
    pallas_call x1, Pallas kernels, shards(): pl.pallas_call(functools.partial(kernel, n, plane), out_shape=jax.ShapeDt...  46.2 us
    unnamed x1, local copies, waits for them, and re-layouts  2.3 us

profile of v2, /device:TPU:9, one launch (start us, length us, event | category | flops | bytes accessed | tf_op | source)
XLA Modules:
  0.0 48.5 jit_solution(18336765596981632322)
XLA Ops:
  0.0 46.2 %layer.1 = bf16[256,2048]{1,0:T(8,128)(2,1)} custom-call(s32[16]{0:T(128)} %counts_in.1, bf16[256,2,256]{2,1,0:T(2,128)(2,1)} %q_in.1, bf16[256,2,256]{2,1,0:T(2,128)(2,1)} %k_in.1, bf16[256,2,256]{2,1,0:T(2,128)(2,1)} %v_in.1, f32[2,256]{1,0:T(2,128)} %bitcast.1, f32[2,3,256,256]{3,2,1,0:T(8,128)} %fw_in.1, bf16[512,4096]{1,0:T(8,128)(2,1)} %ow.1), custom_call_target="tpu_custom_call" | custom-call | tf_op jit(solution)/shard_map/layer/pallas_call | solution.py:460
  46.2 2.3 %copy.9 = bf16[256,2048]{1,0:T(8,128)(2,1)} copy(bf16[256,2048]{1,0:T(8,128)(2,1)} %layer.1) | data formatting | bytes 2097152
